TPU v7x, 32 devices: a whole 2x2x4 slice. The times are simulated.
32 devices in a mesh: dp: 4 (over y, x), shard: 8 (over z, core).
Axes of the slice: x: 2, y: 2, z: 4, core: 2. Of those that a mesh axis runs over, the one named last changes fastest.
Arguments:
- grads: float32 [4, 1, 2, 4096, 4096], P('dp', None, None, None, 'shard'), may hold values from -6 to 6
- params: float32 [1, 2, 4096, 4096], P(None, None, ('dp', 'shard')), may hold values from -0.09375 to 0.09375
- moment_one: float32 [1, 2, 4096, 4096], P(None, None, ('dp', 'shard')), may hold values from -0.75 to 0.75
- moment_two: float32 [1, 2, 4096, 4096], P(None, None, ('dp', 'shard')), may hold values from 1e-05 to 0.01
- relation_ids: int32 [1], replicated, may hold values from 0 to 63
- rates: float32 [64], replicated, may hold values from 0.02 to 0.1
- step_count: int32 [1], replicated, may hold values from 1 to 8
Outputs:
- new_params: float32 [1, 2, 4096, 4096], P(None, None, ('dp', 'shard'))
- new_moment_one: float32 [1, 2, 4096, 4096], P(None, None, ('dp', 'shard'))
- new_moment_two: float32 [1, 2, 4096, 4096], P(None, None, ('dp', 'shard'))
- panels: bfloat16 [1, 2, 4096, 4096], P(None, None, None, 'shard')
Inputs may be any that keep to these rules, and one draw needn't show every extreme that they name: `relation_ids`: relation ids are edge types. `step_count`: the step count is positive.
All inputs are finite; a program needn't handle non-finite values.
Results may differ from a plain program's by a relative error of at most 0.001.
Values may be sent and summed in bfloat16 or wider, within the bound.
A program may use at most 128 MiB of HBM per device.

v0:
```python
import functools
import math

import jax
import jax.numpy as jnp
from jax import lax
from jax.experimental import pallas as pl
from jax.experimental.pallas import tpu as pltpu
from jax.sharding import PartitionSpec as P

LIMIT = 6.0
TOP = 32700.0
MESH = pl.DeviceIdType.MESH
LAGS = (0, 2, 3, 4, 5, 6)
ROWS = 32


def encode(x, limit):
    root = x * lax.rsqrt(jnp.abs(x) + 1e-30) * (TOP / math.sqrt(limit))
    return jnp.round(root).astype(jnp.int32).astype(jnp.int16)


def decode(code, limit):
    root = code.astype(jnp.int32).astype(jnp.float32)
    return root * jnp.abs(root) * (limit / TOP**2)


def kernel(sizes, scal, grads, params, mone, mtwo, o_p, o_1, o_2, panels,
           gb, vp, v1, v2, c1, r1, c2, r2, r3, pan,
           g_sem, in_sem, out_sem, own_sem, s1s, s1r, s2s, s2r, s3s, s3r, s4s, s4r, s5s, s5r, s6s, s6r):
    na, nb, n_sh, mats, relations, rows, splits, pc = sizes
    n_dp = na * nb
    chunks = mats * splits
    dpi = lax.axis_index("dp")
    me = lax.axis_index("shard")
    a, b = dpi // nb, dpi % nb

    def geometry(k):
        m, c = k // splits, k % splits
        return m, pl.ds(c * rows, rows)

    def dims(k):
        if k % 2 == 0:
            return na, nb, a, b, lambda f, g: f * nb + g
        return nb, na, b, a, lambda f, g: g * nb + f

    def load(k):
        m, r = geometry(k)
        nf, ng = dims(k)[:2]
        for f in range(nf):
            if k % 2 == 0:
                src = grads.at[m, f, :, :, r, :]
            else:
                src = grads.at[m, :, f, :, r, :]
            pltpu.make_async_copy(src, gb.at[k, pl.ds(f * ng, ng)], g_sem.at[k]).start()
        for i, (src, dst) in enumerate(((params, vp), (mone, v1), (mtwo, v2))):
            pltpu.make_async_copy(src.at[m, r, :], dst.at[k], in_sem.at[i, k]).start()

    def remote(src, dst, ss, rs, dp, sh):
        return pltpu.make_async_remote_copy(
            src_ref=src, dst_ref=dst, send_sem=ss, recv_sem=rs,
            device_id=(dp, sh), device_id_type=MESH)

    def one(k, j):
        nf, ng, f, g, flat = dims(k)
        part = pl.ds((j - 1) * ng, ng)
        return remote(c1.at[k, part], r1.at[k, part], s1s.at[k, j - 1], s1r.at[k, j - 1],
                      flat((f + j) % nf, g), me)

    def two(k, j):
        nf, ng, f, g, flat = dims(k)
        return remote(c2.at[k, j - 1], r2.at[k, j - 1], s2s.at[k, j - 1], s2r.at[k, j - 1],
                      flat(f, (g + j) % ng), me)

    def stage0(k):
        nf, ng, f, g, flat = dims(k)
        pltpu.make_async_copy(gb.at[k], gb.at[k], g_sem.at[k]).wait()
        for j in range(1, nf):
            to = (f + j) % nf

            def body(i, _):
                for h in range(ng):
                    c1[k, (j - 1) * ng + h, i] = encode(gb[k, to * ng + h, i], LIMIT)
                return 0

            lax.fori_loop(0, n_sh, body, 0)
            one(k, j).start()

    def stage1(k):
        nf, ng, f, g, flat = dims(k)
        for j in range(1, nf):
            one(k, j).wait_recv()

        def total(h, i):
            value = gb[k, f * ng + h, i]
            for j in range(1, nf):
                value = value + decode(r1[k, (j - 1) * ng + h, i], LIMIT)
            return value

        for j in range(1, ng):
            to = (g + j) % ng

            def body(i, _):
                c2[k, j - 1, i] = encode(total(to, i), LIMIT * nf)
                return 0

            lax.fori_loop(0, n_sh, body, 0)
            two(k, j).start()

        def own(i, _):
            gb[k, f * ng + g, i] = total(g, i)
            return 0

        lax.fori_loop(0, n_sh, own, 0)

    def stage2(k):
        nf, ng, f, g, flat = dims(k)
        for j in range(1, ng):
            two(k, j).wait_recv()

        def body(i, _):
            value = gb[k, f * ng + g, i]
            for j in range(1, ng):
                value = value + decode(r2[k, j - 1, i], LIMIT * nf)
            gb[k, f * ng + g, i] = value
            return 0

        lax.fori_loop(0, n_sh, body, 0)

        def send(j, _):
            to = (me + j) % n_sh
            remote(gb.at[k, f * ng + g, to], r3.at[k, j - 1], s3s.at[k], s3r.at[k], dpi, to).start()
            return 0

        lax.fori_loop(1, n_sh, send, 0)

    def stage3(k):
        m, r = geometry(k)
        nf, ng, f, g, flat = dims(k)
        some = r3.at[k]
        pltpu.make_async_copy(some, some, s3r.at[k]).wait()
        for i, dst in enumerate((vp, v1, v2)):
            pltpu.make_async_copy(dst.at[k], dst.at[k], in_sem.at[i, k]).wait()
        rel = m // (mats // relations)
        learn = scal[2 + rel]
        inv_one, inv_two = scal[0], scal[1]

        def update(total, s):
            cols = pl.ds(pl.multiple_of(s * pc, 128), pc)
            gradient = total * (1.0 / n_dp)
            p = vp[k, :, cols]
            new_one = 0.9 * v1[k, :, cols] + 0.1 * gradient
            new_two = 0.95 * v2[k, :, cols] + 0.05 * gradient * gradient
            step = (new_one * inv_one) / (jnp.sqrt(new_two * inv_two) + 1e-08) + 0.1 * p
            new_p = p - learn * step
            vp[k, :, cols] = new_p
            v1[k, :, cols] = new_one
            v2[k, :, cols] = new_two
            pan[k, s] = new_p.astype(jnp.bfloat16)

        def body(j, _):
            s = (me + n_sh - j) % n_sh
            update(r3[k, j - 1], s)
            remote(pan.at[k, s], panels.at[m, a, b, me, r, :], s4s.at[k], s4r.at[k], dpi, s).start()
            return 0

        lax.fori_loop(1, n_sh, body, 0)
        update(gb[k, f * ng + g, me], me)
        pltpu.make_async_copy(pan.at[k, me], panels.at[m, a, b, me, r, :], own_sem.at[k]).start()
        for i, (src, dst) in enumerate(((vp, o_p), (v1, o_1), (v2, o_2))):
            pltpu.make_async_copy(src.at[k], dst.at[m, r, :], out_sem.at[i, k]).start()

    def five(k, j, came=False):
        m, r = geometry(k)
        nf, ng, f, g, flat = dims(k)
        block = panels.at[m, a, b, :, r, :]
        return remote(block, block, s5s.at[k, j - 1], s5r.at[k, j - 1], flat((f + j) % nf, g), me)

    def stage4(k):
        m, r = geometry(k)
        nf = dims(k)[0]
        some = panels.at[m, a, b, pl.ds(0, n_sh - 1), r, :]
        pltpu.make_async_copy(some, some, s4r.at[k]).wait()
        pltpu.make_async_copy(pan.at[k, me], panels.at[m, a, b, me, r, :], own_sem.at[k]).wait()
        for j in range(1, nf):
            five(k, j).start()

    def six(k, j):
        m, r = geometry(k)
        nf, ng, f, g, flat = dims(k)
        block = panels.at[m, :, b, :, r, :] if k % 2 == 0 else panels.at[m, a, :, :, r, :]
        return remote(block, block, s6s.at[k, j - 1], s6r.at[k, j - 1], flat(f, (g + j) % ng), me)

    def stage5(k):
        nf, ng = dims(k)[:2]
        for j in range(1, nf):
            five(k, j).wait_recv()
        for j in range(1, ng):
            six(k, j).start()

    for k in range(chunks):
        load(k)

    barrier = pltpu.get_barrier_semaphore()
    for j in range(1, na):
        pl.semaphore_signal(barrier, inc=1, device_id=(((a + j) % na) * nb + b, me), device_id_type=MESH)
    for j in range(1, nb):
        pl.semaphore_signal(barrier, inc=1, device_id=(a * nb + (b + j) % nb, me), device_id_type=MESH)
    for j in range(1, n_sh):
        pl.semaphore_signal(barrier, inc=1, device_id=(dpi, (me + j) % n_sh), device_id_type=MESH)
    pl.semaphore_wait(barrier, na - 1 + nb - 1 + n_sh - 1)

    stages = (stage0, stage1, stage2, stage3, stage4, stage5)
    for t in range(chunks + LAGS[-1]):
        for n in (0, 5, 4, 3, 2, 1):
            k = t - LAGS[n]
            if 0 <= k < chunks:
                stages[n](k)

    for k in range(chunks):
        m, r = geometry(k)
        nf, ng = dims(k)[:2]
        for j in range(1, nf):
            one(k, j).wait_send()
            five(k, j).wait_send()
        for j in range(1, ng):
            two(k, j).wait_send()
            six(k, j).wait_send()
            six(k, j).wait_recv()
        some = r3.at[k]
        pltpu.make_async_copy(some, some, s3s.at[k]).wait()
        some = pan.at[k, pl.ds(0, n_sh - 1)]
        pltpu.make_async_copy(some, some, s4s.at[k]).wait()
        for i, (src, dst) in enumerate(((vp, o_p), (v1, o_1), (v2, o_2))):
            pltpu.make_async_copy(src.at[k], dst.at[m, r, :], out_sem.at[i, k]).wait()


def body(grads, params, moment_one, moment_two, relation_ids, rates, step_count):
    n_dp = lax.axis_size("dp")
    n_sh = lax.axis_size("shard")
    relations = grads.shape[1]
    mats = relations * 2
    pc = grads.shape[-1]
    width = pc * n_sh
    owned = params.shape[2]
    nb = 2 if n_dp % 2 == 0 else 1
    na = n_dp // nb
    rows = min(ROWS, owned)
    splits = owned // rows
    chunks = mats * splits
    onehot = (relation_ids[:, None] == jnp.arange(rates.shape[0], dtype=jnp.int32)[None, :]).astype(
        jnp.float32
    )
    learn = jnp.sum(onehot * rates[None, :], axis=1)
    steps = step_count[0].astype(jnp.float32)
    fix_one = 1.0 - jnp.power(jnp.float32(0.9), steps)
    fix_two = 1.0 - jnp.power(jnp.float32(0.95), steps)
    scal = jnp.concatenate([jnp.stack([1.0 / fix_one, 1.0 / fix_two]), learn])
    pieces = grads.reshape(mats, na, nb, n_sh, owned, pc)
    flat = [x.reshape(mats, owned, width) for x in (params, moment_one, moment_two)]
    state = jax.ShapeDtypeStruct((mats, owned, width), jnp.float32)
    first = n_dp - min(na, nb)
    second = max(na, nb) - 1
    hand = pl.BlockSpec(memory_space=pl.ANY)
    dma = pltpu.SemaphoreType.DMA
    most = second
    out = pl.pallas_call(
        functools.partial(kernel, (na, nb, n_sh, mats, relations, rows, splits, pc)),
        out_shape=(state, state, state,
                   jax.ShapeDtypeStruct((mats, na, nb, n_sh, owned, pc), jnp.bfloat16)),
        in_specs=[pl.BlockSpec(memory_space=pltpu.SMEM)] + [hand] * 4,
        out_specs=(hand,) * 4,
        scratch_shapes=[
            pltpu.VMEM((chunks, n_dp, n_sh, rows, pc), jnp.float32),
            pltpu.VMEM((chunks, rows, width), jnp.float32),
            pltpu.VMEM((chunks, rows, width), jnp.float32),
            pltpu.VMEM((chunks, rows, width), jnp.float32),
            pltpu.VMEM((chunks, first, n_sh, rows, pc), jnp.int16),
            pltpu.VMEM((chunks, first, n_sh, rows, pc), jnp.int16),
            pltpu.VMEM((chunks, second, n_sh, rows, pc), jnp.int16),
            pltpu.VMEM((chunks, second, n_sh, rows, pc), jnp.int16),
            pltpu.VMEM((chunks, n_sh - 1, rows, pc), jnp.float32),
            pltpu.VMEM((chunks, n_sh, rows, pc), jnp.bfloat16),
            dma((chunks,)),
            dma((3, chunks)),
            dma((3, chunks)),
            dma((chunks,)),
            dma((chunks, most)), dma((chunks, most)),
            dma((chunks, most)), dma((chunks, most)),
            dma((chunks,)), dma((chunks,)),
            dma((chunks,)), dma((chunks,)),
            dma((chunks, most)), dma((chunks, most)),
            dma((chunks, most)), dma((chunks, most)),
        ],
        compiler_params=pltpu.CompilerParams(
            collective_id=0, has_side_effects=True, vmem_limit_bytes=56 * 1024 * 1024),
        cost_estimate=pl.CostEstimate(flops=50 * mats * owned * width, bytes_accessed=56 * mats * owned * width // 1,
                                      transcendentals=0),
    )(scal, pieces, *flat)
    new_params, new_one, new_two = (x.reshape(params.shape) for x in out[:3])
    panels = out[3].reshape(relations, 2, owned * n_sh * n_dp, pc)
    return (new_params, new_one, new_two, panels)


def solution(mesh):
    in_specs = (
        P("dp", None, None, None, "shard"),
        P(None, None, ("dp", "shard"), None),
        P(None, None, ("dp", "shard"), None),
        P(None, None, ("dp", "shard"), None),
        P(),
        P(),
        P(),
    )
    out_specs = (
        P(None, None, ("dp", "shard"), None),
        P(None, None, ("dp", "shard"), None),
        P(None, None, ("dp", "shard"), None),
        P(None, None, None, "shard"),
    )
    return jax.shard_map(body, mesh=mesh, in_specs=in_specs, out_specs=out_specs, check_vma=False)
```

profile of v0, /device:TPU:18, one launch (start us, length us, event | category | flops | bytes accessed | tf_op | source)
XLA Modules:
  0.0 222.1 jit_solution(2384615304408289464)
XLA Ops:
  2.1 1.3 fusion
  3.3 1.2 pad_maximum_fusion.scal
  4.6 199.7 %shard_map.102 = (f32[2,128,4096]{2,1,0:T(8,128)}, f32[2,128,4096]{2,1,0:T(8,128)}, f32[2,128,4096]{2,1,0:T(8,128)}, bf16[2,2,2,8,128,512]{5,4,3,2,1,0:T(8,128)(2,1)}) custom-call(f32[3]{0:T(128)} %pad_maximum_fusion.scal, f32[2,2,2,8,128,512]{5,4,3,2,1,0:T(8,128)} %bitcast.11, f32[2,128,4096]{2,1,0:T(8,128)} %bitcast.16, f32[2,128,4096]{2,1,0:T(8,128)} %bitcast.17, ...), custom_call_target="tpu_custom_call" | custom-call | flops 52428800 | bytes 58720256 | tf_op jit(solution)/shard_map/pallas_call | solution.py:267
  204.3 0.0 copy-start.1
  204.3 4.8 %copy.17 = f32[1,2,128,4096]{3,2,1,0:T(8,128)} copy(f32[1,2,128,4096]{3,2,1,0:T(8,128)} %bitcast.15) | data formatting | bytes 8388608
  209.1 0.0 copy-done.1
  209.1 0.0 copy-start
  209.1 2.1 copy.18
  211.2 1.6 copy-done
  212.8 2.0 copy.19
  214.8 7.3 %copy.20 = bf16[1,2,4096,512]{3,2,1,0:T(8,128)(2,1)} copy(bf16[1,2,4096,512]{3,2,1,0:T(8,128)(2,1)} %bitcast.12) | data formatting | bytes 16777216
Async XLA Ops:
  204.3 4.8 %copy-start.1 = (f32[2,128,4096]{2,1,0:T(8,128)S(1)}, f32[2,128,4096]{2,1,0:T(8,128)}, u32[]{:S(2)}) copy-start(f32[2,128,4096]{2,1,0:T(8,128)} %get-tuple-element.9) | copy-start | bytes 12582916
  209.1 3.7 %copy-start = (f32[2,128,4096]{2,1,0:T(8,128)S(1)}, f32[2,128,4096]{2,1,0:T(8,128)}, u32[]{:S(2)}) copy-start(f32[2,128,4096]{2,1,0:T(8,128)} %get-tuple-element.10) | copy-start | bytes 12582916
where the time goes:
time: 222 us
  Pallas kernels  200 us (90%)
  local copies, waits for them, and re-layouts  17.8 us (8%)
  other arithmetic  2.49 us (1%)
    pallas_call x1, Pallas kernels, body(): pl.pallas_call(functools.partial(kernel, (na, nb, n_sh, mats, relations,...  200 us
    unnamed x8, local copies, waits for them, and re-layouts  17.8 us

commit v1 on v0

--- a/solution.py
+++ b/solution.py
@@ -10,19 +10,24 @@
 
 LIMIT = 6.0
 TOP = 32700.0
+SOFT = 0.61
 MESH = pl.DeviceIdType.MESH
-LAGS = (0, 2, 3, 4, 5, 6)
-ROWS = 32
+LAGS = (0, 2, 4, 6, 8, 10)
+ROWS = 16
 
 
 def encode(x, limit):
-    root = x * lax.rsqrt(jnp.abs(x) + 1e-30) * (TOP / math.sqrt(limit))
-    return jnp.round(root).astype(jnp.int32).astype(jnp.int16)
+    soft = SOFT * math.sqrt(limit)
+    scale = TOP * math.sqrt(limit**2 + soft**2) / limit
+    bent = x * lax.rsqrt(x * x + soft**2) * scale
+    return jnp.round(bent).astype(jnp.int32).astype(jnp.int16)
 
 
 def decode(code, limit):
-    root = code.astype(jnp.int32).astype(jnp.float32)
-    return root * jnp.abs(root) * (limit / TOP**2)
+    soft = SOFT * math.sqrt(limit)
+    scale = TOP * math.sqrt(limit**2 + soft**2) / limit
+    bent = code.astype(jnp.int32).astype(jnp.float32) * (1.0 / scale)
+    return bent * lax.rsqrt(1.0 - bent * bent) * soft
 
 
 def kernel(sizes, scal, grads, params, mone, mtwo, o_p, o_1, o_2, panels,

time: 222 us -> 195 us (0.88)
  the two profiles are of different devices: /device:TPU:18 before, /device:TPU:0 now
where the time goes in v1:
time: 195 us
  Pallas kernels  172 us (88%)
  local copies, waits for them, and re-layouts  17.8 us (9%)
  other arithmetic  2.49 us (1%)
  between operations  2.11 us (1%)
    pallas_call x1, Pallas kernels, body(): pl.pallas_call(functools.partial(kernel, (na, nb, n_sh, mats, relations,...  172 us
    unnamed x8, local copies, waits for them, and re-layouts  17.8 us

profile of v1, /device:TPU:0, one launch (start us, length us, event | category | flops | bytes accessed | tf_op | source)
XLA Modules:
  0.0 194.9 jit_solution(12074160932300028384)
XLA Ops:
  2.1 1.3 fusion
  3.3 1.2 pad_maximum_fusion.scal
  4.6 172.4 %shard_map.102 = (f32[2,128,4096]{2,1,0:T(8,128)}, f32[2,128,4096]{2,1,0:T(8,128)}, f32[2,128,4096]{2,1,0:T(8,128)}, bf16[2,2,2,8,128,512]{5,4,3,2,1,0:T(8,128)(2,1)}) custom-call(f32[3]{0:T(128)} %pad_maximum_fusion.scal, f32[2,2,2,8,128,512]{5,4,3,2,1,0:T(8,128)} %bitcast.11, f32[2,128,4096]{2,1,0:T(8,128)} %bitcast.16, f32[2,128,4096]{2,1,0:T(8,128)} %bitcast.17, ...), custom_call_target="tpu_custom_call" | custom-call | flops 52428800 | bytes 58720256 | tf_op jit(solution)/shard_map/pallas_call | solution.py:272
  177.0 0.0 copy-start.1
  177.0 4.8 %copy.17 = f32[1,2,128,4096]{3,2,1,0:T(8,128)} copy(f32[1,2,128,4096]{3,2,1,0:T(8,128)} %bitcast.15) | data formatting | bytes 8388608
  181.8 0.0 copy-done.1
  181.9 0.0 copy-start
  181.9 2.1 %copy.18 = f32[1,2,128,4096]{3,2,1,0:T(8,128)} copy(f32[1,2,128,4096]{3,2,1,0:T(8,128)S(1)} %bitcast.14) | data formatting | bytes 8388608
  184.0 1.6 copy-done
  185.6 2.0 %copy.19 = f32[1,2,128,4096]{3,2,1,0:T(8,128)} copy(f32[1,2,128,4096]{3,2,1,0:T(8,128)S(1)} %bitcast.13) | data formatting | bytes 8388608
  187.6 7.3 %copy.20 = bf16[1,2,4096,512]{3,2,1,0:T(8,128)(2,1)} copy(bf16[1,2,4096,512]{3,2,1,0:T(8,128)(2,1)} %bitcast.12) | data formatting | bytes 16777216
Async XLA Ops:
  177.0 4.8 %copy-start.1 = (f32[2,128,4096]{2,1,0:T(8,128)S(1)}, f32[2,128,4096]{2,1,0:T(8,128)}, u32[]{:S(2)}) copy-start(f32[2,128,4096]{2,1,0:T(8,128)} %get-tuple-element.9) | copy-start | bytes 12582916
  181.9 3.7 %copy-start = (f32[2,128,4096]{2,1,0:T(8,128)S(1)}, f32[2,128,4096]{2,1,0:T(8,128)}, u32[]{:S(2)}) copy-start(f32[2,128,4096]{2,1,0:T(8,128)} %get-tuple-element.10) | copy-start | bytes 12582916

commit v2 on v1

--- a/solution.py
+++ b/solution.py
@@ -31,7 +31,7 @@
 
 
 def kernel(sizes, scal, grads, params, mone, mtwo, o_p, o_1, o_2, panels,
-           gb, vp, v1, v2, c1, r1, c2, r2, r3, pan,
+           gb, vp, v1, v2, c1, r1, c2, r2, c3, r3, pan,
            g_sem, in_sem, out_sem, own_sem, s1s, s1r, s2s, s2r, s3s, s3r, s4s, s4r, s5s, s5r, s6s, s6r):
     na, nb, n_sh, mats, relations, rows, splits, pc = sizes
     n_dp = na * nb
@@ -128,13 +128,14 @@
             for j in range(1, ng):
                 value = value + decode(r2[k, j - 1, i], LIMIT * nf)
             gb[k, f * ng + g, i] = value
+            c3[k, i] = encode(value, LIMIT * n_dp)
             return 0
 
         lax.fori_loop(0, n_sh, body, 0)
 
         def send(j, _):
             to = (me + j) % n_sh
-            remote(gb.at[k, f * ng + g, to], r3.at[k, j - 1], s3s.at[k], s3r.at[k], dpi, to).start()
+            remote(c3.at[k, to], r3.at[k, j - 1], s3s.at[k], s3r.at[k], dpi, to).start()
             return 0
 
         lax.fori_loop(1, n_sh, send, 0)
@@ -165,7 +166,7 @@
 
         def body(j, _):
             s = (me + n_sh - j) % n_sh
-            update(r3[k, j - 1], s)
+            update(decode(r3[k, j - 1], LIMIT * n_dp), s)
             remote(pan.at[k, s], panels.at[m, a, b, me, r, :], s4s.at[k], s4r.at[k], dpi, s).start()
             return 0
 
@@ -284,7 +285,8 @@
             pltpu.VMEM((chunks, first, n_sh, rows, pc), jnp.int16),
             pltpu.VMEM((chunks, second, n_sh, rows, pc), jnp.int16),
             pltpu.VMEM((chunks, second, n_sh, rows, pc), jnp.int16),
-            pltpu.VMEM((chunks, n_sh - 1, rows, pc), jnp.float32),
+            pltpu.VMEM((chunks, n_sh, rows, pc), jnp.int16),
+            pltpu.VMEM((chunks, n_sh - 1, rows, pc), jnp.int16),
             pltpu.VMEM((chunks, n_sh, rows, pc), jnp.bfloat16),
             dma((chunks,)),
             dma((3, chunks)),

time: 195 us -> 172 us (0.88)
  Pallas kernels: 172 us -> 150 us
    pallas_call x1, Pallas kernels: 172 us -> 150 us  [body(): pl.pallas_call(functools.partial(kernel, (na, nb, n_sh, mats, relations,...]
where the time goes in v2:
time: 172 us
  Pallas kernels  150 us (87%)
  local copies, waits for them, and re-layouts  17.8 us (10%)
  other arithmetic  2.49 us (1%)
  between operations  2.11 us (1%)
    pallas_call x1, Pallas kernels, body(): pl.pallas_call(functools.partial(kernel, (na, nb, n_sh, mats, relations,...  150 us
    unnamed x8, local copies, waits for them, and re-layouts  17.8 us

profile of v2, /device:TPU:0, one launch (start us, length us, event | category | flops | bytes accessed | tf_op | source)
XLA Modules:
  0.0 172.2 jit_solution(16901162533792064150)
XLA Ops:
  2.1 1.3 fusion
  3.3 1.2 pad_maximum_fusion.scal
  4.6 149.8 %shard_map.102 = (f32[2,128,4096]{2,1,0:T(8,128)}, f32[2,128,4096]{2,1,0:T(8,128)}, f32[2,128,4096]{2,1,0:T(8,128)}, bf16[2,2,2,8,128,512]{5,4,3,2,1,0:T(8,128)(2,1)}) custom-call(f32[3]{0:T(128)} %pad_maximum_fusion.scal, f32[2,2,2,8,128,512]{5,4,3,2,1,0:T(8,128)} %bitcast.11, f32[2,128,4096]{2,1,0:T(8,128)} %bitcast.16, f32[2,128,4096]{2,1,0:T(8,128)} %bitcast.17, ...), custom_call_target="tpu_custom_call" | custom-call | flops 52428800 | bytes 58720256 | tf_op jit(solution)/shard_map/pallas_call | solution.py:273
  154.4 0.0 copy-start.1
  154.4 4.8 %copy.17 = f32[1,2,128,4096]{3,2,1,0:T(8,128)} copy(f32[1,2,128,4096]{3,2,1,0:T(8,128)} %bitcast.15) | data formatting | bytes 8388608
  159.2 0.0 copy-done.1
  159.2 0.0 copy-start
  159.2 2.1 %copy.18 = f32[1,2,128,4096]{3,2,1,0:T(8,128)} copy(f32[1,2,128,4096]{3,2,1,0:T(8,128)S(1)} %bitcast.14) | data formatting | bytes 8388608
  161.3 1.6 copy-done
  162.9 2.0 %copy.19 = f32[1,2,128,4096]{3,2,1,0:T(8,128)} copy(f32[1,2,128,4096]{3,2,1,0:T(8,128)S(1)} %bitcast.13) | data formatting | bytes 8388608
  164.9 7.3 %copy.20 = bf16[1,2,4096,512]{3,2,1,0:T(8,128)(2,1)} copy(bf16[1,2,4096,512]{3,2,1,0:T(8,128)(2,1)} %bitcast.12) | data formatting | bytes 16777216
Async XLA Ops:
  154.4 4.8 %copy-start.1 = (f32[2,128,4096]{2,1,0:T(8,128)S(1)}, f32[2,128,4096]{2,1,0:T(8,128)}, u32[]{:S(2)}) copy-start(f32[2,128,4096]{2,1,0:T(8,128)} %get-tuple-element.9) | copy-start | bytes 12582916
  159.2 3.7 %copy-start = (f32[2,128,4096]{2,1,0:T(8,128)S(1)}, f32[2,128,4096]{2,1,0:T(8,128)}, u32[]{:S(2)}) copy-start(f32[2,128,4096]{2,1,0:T(8,128)} %get-tuple-element.10) | copy-start | bytes 12582916

commit v3 on v2

--- a/solution.py
+++ b/solution.py
@@ -30,7 +30,7 @@
     return bent * lax.rsqrt(1.0 - bent * bent) * soft
 
 
-def kernel(sizes, scal, grads, params, mone, mtwo, o_p, o_1, o_2, panels,
+def kernel(sizes, ids, rates, count, grads, params, mone, mtwo, o_p, o_1, o_2, panels,
            gb, vp, v1, v2, c1, r1, c2, r2, c3, r3, pan,
            g_sem, in_sem, out_sem, own_sem, s1s, s1r, s2s, s2r, s3s, s3r, s4s, s4r, s5s, s5r, s6s, s6r):
     na, nb, n_sh, mats, relations, rows, splits, pc = sizes
@@ -148,8 +148,10 @@
         for i, dst in enumerate((vp, v1, v2)):
             pltpu.make_async_copy(dst.at[k], dst.at[k], in_sem.at[i, k]).wait()
         rel = m // (mats // relations)
-        learn = scal[2 + rel]
-        inv_one, inv_two = scal[0], scal[1]
+        learn = rates[ids[rel]]
+        steps = jnp.full((1, pc), count[0].astype(jnp.float32))
+        inv_one = 1.0 / (1.0 - jnp.exp(steps * math.log(0.9)))
+        inv_two = 1.0 / (1.0 - jnp.exp(steps * math.log(0.95)))
 
         def update(total, s):
             cols = pl.ds(pl.multiple_of(s * pc, 128), pc)
@@ -254,14 +256,6 @@
     rows = min(ROWS, owned)
     splits = owned // rows
     chunks = mats * splits
-    onehot = (relation_ids[:, None] == jnp.arange(rates.shape[0], dtype=jnp.int32)[None, :]).astype(
-        jnp.float32
-    )
-    learn = jnp.sum(onehot * rates[None, :], axis=1)
-    steps = step_count[0].astype(jnp.float32)
-    fix_one = 1.0 - jnp.power(jnp.float32(0.9), steps)
-    fix_two = 1.0 - jnp.power(jnp.float32(0.95), steps)
-    scal = jnp.concatenate([jnp.stack([1.0 / fix_one, 1.0 / fix_two]), learn])
     pieces = grads.reshape(mats, na, nb, n_sh, owned, pc)
     flat = [x.reshape(mats, owned, width) for x in (params, moment_one, moment_two)]
     state = jax.ShapeDtypeStruct((mats, owned, width), jnp.float32)
@@ -274,7 +268,7 @@
         functools.partial(kernel, (na, nb, n_sh, mats, relations, rows, splits, pc)),
         out_shape=(state, state, state,
                    jax.ShapeDtypeStruct((mats, na, nb, n_sh, owned, pc), jnp.bfloat16)),
-        in_specs=[pl.BlockSpec(memory_space=pltpu.SMEM)] + [hand] * 4,
+        in_specs=[pl.BlockSpec(memory_space=pltpu.SMEM)] * 3 + [hand] * 4,
         out_specs=(hand,) * 4,
         scratch_shapes=[
             pltpu.VMEM((chunks, n_dp, n_sh, rows, pc), jnp.float32),
@@ -303,7 +297,7 @@
             collective_id=0, has_side_effects=True, vmem_limit_bytes=56 * 1024 * 1024),
         cost_estimate=pl.CostEstimate(flops=50 * mats * owned * width, bytes_accessed=56 * mats * owned * width // 1,
                                       transcendentals=0),
-    )(scal, pieces, *flat)
+    )(relation_ids, rates, step_count, pieces, *flat)
     new_params, new_one, new_two = (x.reshape(params.shape) for x in out[:3])
     panels = out[3].reshape(relations, 2, owned * n_sh * n_dp, pc)
     return (new_params, new_one, new_two, panels)

time: 172 us -> 170 us (0.988)
  other arithmetic: 2.49 us -> 0 us
where the time goes in v3:
time: 170 us
  Pallas kernels  150 us (88%)
  local copies, waits for them, and re-layouts  17.8 us (10%)
  between operations  1.94 us (1%)
    pallas_call x1, Pallas kernels, body(): pl.pallas_call(functools.partial(kernel, (na, nb, n_sh, mats, relations,...  150 us
    unnamed x8, local copies, waits for them, and re-layouts  17.8 us

profile of v3, /device:TPU:0, one launch (start us, length us, event | category | flops | bytes accessed | tf_op | source)
XLA Modules:
  0.0 169.6 jit_solution(9229346867940332048)
XLA Ops:
  1.9 149.8 %shard_map.102 = (f32[2,128,4096]{2,1,0:T(8,128)}, f32[2,128,4096]{2,1,0:T(8,128)}, f32[2,128,4096]{2,1,0:T(8,128)}, bf16[2,2,2,8,128,512]{5,4,3,2,1,0:T(8,128)(2,1)}) custom-call(s32[1]{0:T(128)S(6)} %copy.15.ids, f32[64]{0:T(128)} %rates.1, s32[1]{0:T(128)S(6)} %copy.16.count, f32[2,2,2,8,128,512]{5,4,3,2,1,0:T(8,128)} %bitcast.8, ...), custom_call_target="tpu_custom_call" | custom-call | flops 52428800 | bytes 58720256 | tf_op jit(solution)/shard_map/pallas_call | solution.py:267
  151.7 0.0 copy-start.1
  151.7 4.8 %copy.17 = f32[1,2,128,4096]{3,2,1,0:T(8,128)} copy(f32[1,2,128,4096]{3,2,1,0:T(8,128)} %bitcast.15) | data formatting | bytes 8388608
  156.6 0.0 copy-done.1
  156.6 0.0 copy-start
  156.6 2.1 %copy.18 = f32[1,2,128,4096]{3,2,1,0:T(8,128)} copy(f32[1,2,128,4096]{3,2,1,0:T(8,128)S(1)} %bitcast.14) | data formatting | bytes 8388608
  158.7 1.6 copy-done
  160.3 2.0 %copy.19 = f32[1,2,128,4096]{3,2,1,0:T(8,128)} copy(f32[1,2,128,4096]{3,2,1,0:T(8,128)S(1)} %bitcast.13) | data formatting | bytes 8388608
  162.3 7.3 %copy.20 = bf16[1,2,4096,512]{3,2,1,0:T(8,128)(2,1)} copy(bf16[1,2,4096,512]{3,2,1,0:T(8,128)(2,1)} %bitcast.9) | data formatting | bytes 16777216
Async XLA Ops:
  151.7 4.8 %copy-start.1 = (f32[2,128,4096]{2,1,0:T(8,128)S(1)}, f32[2,128,4096]{2,1,0:T(8,128)}, u32[]{:S(2)}) copy-start(f32[2,128,4096]{2,1,0:T(8,128)} %get-tuple-element.9) | copy-start | bytes 12582916
  156.6 3.7 %copy-start = (f32[2,128,4096]{2,1,0:T(8,128)S(1)}, f32[2,128,4096]{2,1,0:T(8,128)}, u32[]{:S(2)}) copy-start(f32[2,128,4096]{2,1,0:T(8,128)} %get-tuple-element.10) | copy-start | bytes 12582916
